TPU v7x, 32 devices: a whole 2x2x4 slice. The times are simulated.
32 devices in a mesh: member: 2 (over x), lon: 16 (over z, y, core).
Axes of the slice: x: 2, y: 2, z: 4, core: 2. Of those that a mesh axis runs over, the one named last changes fastest.
Arguments:
- surface_old: float32 [1024, 256], P(('member', 'lon')), parts along dimension 0, may hold values from -6 to 6
- surface_forcing: float32 [1024, 256], P(('member', 'lon')), parts along dimension 0, may hold values from -13 to 13
- surface_coeff: float32 [512, 256], P('lon'), may hold values from 0.1 to 1
- ocean_mask: int32 [512, 256], P('lon'), may hold values from 0 to 1, as said below
- column_depth: int32 [256, 512], P('lon'), may hold values from 0 to 16, as said below
- east_depth: int32 [256, 512], P('lon'), may hold values from 0 to 16, as said below
- tracers: float32 [16, 16, 256, 512], P('member', None, 'lon'), parts along dimension 0, may hold values from 0.05 to 2
- u_clinic: float32 [32, 256, 512], P('member', 'lon'), parts along dimension 0, may hold values from -0.9 to 0.9
- v_clinic: float32 [32, 256, 512], P('member', 'lon'), parts along dimension 0, may hold values from -0.9 to 0.9
Outputs:
- surface: float32 [1024, 256], P(('member', 'lon')), parts along dimension 0
- tracers_new: float32 [16, 16, 256, 512], P('member', None, 'lon'), parts along dimension 0
There are 2 independent parts, one for each index of `member`. A program takes and returns all parts, laid end to end along the dimension named above; an argument that names none is the same for every part. Nothing has to cross between parts.
Inputs may be any that keep to these rules, and one draw needn't show every extreme that they name: ocean_mask[j, i] is 1 exactly where column_depth[i, j] is positive, else 0. `column_depth`: 0 marks land. east_depth[i, j] is the smaller of column_depth[i, j] and column_depth[i + 1, j], longitudes periodic.
All inputs are finite; a program needn't handle non-finite values.
Results may differ from a plain program's by a relative error of at most 0.0003.
Values sent between devices are 32-bit elements; how exact they have to be, the bound alone decides.
A program may use at most 64 MiB of HBM per device.

v0:
```python
import jax
import jax.numpy as jnp
from jax import lax
from jax.sharding import PartitionSpec as P

SOLVER_ITERS = 4
BARO_GAIN = 0.1
HORIZ_DIFF = 0.1
VERT_DIFF = 0.15
RATE_CARBON = 0.3
RATE_AMMONIUM = 0.2
RATE_NITRITE = 0.2
RATE_SULFIDE = 0.3
RATE_NITROUS = 0.2
HALF_OXYGEN = 0.3
HALF_NITRATE = 0.3
HALF_NITRITE = 0.3
YIELD_NITROUS = 0.3


def padded_2(block, sides, width, periodic):
    for axis, dim in sides:
        count = lax.axis_size(axis)
        forward = [(i, i + 1) for i in range(count - 1)]
        if periodic:
            forward.append((count - 1, 0))
        backward = [(target, source) for source, target in forward]
        low = lax.ppermute(
            lax.slice_in_dim(block, block.shape[dim] - width, None, axis=dim), axis, forward
        )
        high = lax.ppermute(lax.slice_in_dim(block, 0, width, axis=dim), axis, backward)
        block = jnp.concatenate([low, block, high], axis=dim)
    return block


def apply_operator(values_in, mask_float, coeff):
    masked = mask_float * values_in
    padded = padded_2(masked, (("lon", 0),), 1, False)
    top_device = lax.axis_index("lon") == lax.axis_size("lon") - 1
    folded = jnp.where(top_device, masked[-1:, ::-1], padded[-1:])
    northern = jnp.concatenate([padded[2:-1], folded], axis=0)
    southern = padded[:-2]
    eastern = jnp.roll(masked, -1, axis=1)
    western = jnp.roll(masked, 1, axis=1)
    return (coeff + 4.0 * mask_float) * values_in - mask_float * (
        northern + southern + eastern + western
    )


def squared_total(residual):
    return lax.psum(jnp.sum(residual * residual), "lon")


def plain_solve(right_side, mask_float, coeff):
    solution = jnp.zeros_like(right_side)
    residual = right_side
    direction = right_side
    norm_now = squared_total(residual)
    for sweep in range(SOLVER_ITERS):
        applied = apply_operator(direction, mask_float, coeff)
        curvature = lax.psum(jnp.sum(direction * applied), "lon")
        step_size = norm_now / curvature
        solution = solution + step_size * direction
        residual = residual - step_size * applied
        norm_next = squared_total(residual)
        direction = residual + norm_next / norm_now * direction
        norm_now = norm_next
    return solution


def open_faces(column_depth, east_depth, east_baro, north_baro, u_clinic, v_clinic):
    level_index = lax.broadcasted_iota(jnp.int32, u_clinic.shape, 0)
    wet = (level_index < column_depth[None]).astype(jnp.float32)
    east_open = (level_index < east_depth[None]).astype(jnp.float32)
    north_open = wet * jnp.concatenate([wet[:, :, 1:], jnp.zeros_like(wet[:, :, :1])], axis=2)
    below_open = wet * jnp.concatenate([wet[1:], jnp.zeros_like(wet[:1])], axis=0)
    east_flow = (u_clinic + east_baro[None]) * east_open
    north_flow = (v_clinic + north_baro[None]) * north_open
    return (wet, east_open, north_open, below_open, east_flow, north_flow)


def meridional_vertical(masked, north_flow, north_open, below_open):
    count_rows = masked.shape[-1]
    pad_widths = [(0, 0)] * (masked.ndim - 1) + [(2, 2)]
    padded = jnp.pad(masked, pad_widths)
    south_one = padded[..., 1 : count_rows + 1]
    north_one = padded[..., 3 : count_rows + 3]
    north_two = padded[..., 4 : count_rows + 4]
    face_north = (7.0 * (masked + north_one) - (south_one + north_two)) / 12.0
    flux_north = north_flow * face_north - HORIZ_DIFF * (north_one - masked) * north_open
    flux_south = jnp.concatenate(
        [jnp.zeros_like(flux_north[..., :1]), flux_north[..., :-1]], axis=-1
    )
    below = jnp.concatenate([masked[..., 1:, :, :], jnp.zeros_like(masked[..., :1, :, :])], axis=-3)
    flux_down = VERT_DIFF * (below - masked) * below_open
    flux_up = jnp.concatenate(
        [jnp.zeros_like(flux_down[..., :1, :, :]), flux_down[..., :-1, :, :]], axis=-3
    )
    return flux_south - flux_north + (flux_down - flux_up)


def redox_sources(masked):
    oxygen = masked[0]
    nitrate = masked[1]
    nitrite = masked[2]
    ammonium = masked[3]
    carbon = masked[5]
    sulfide = masked[6]
    nitrous = masked[7]
    breakdown = RATE_CARBON * carbon
    with_oxygen = oxygen / (oxygen + HALF_OXYGEN)
    with_nitrate = (1.0 - with_oxygen) * nitrate / (nitrate + HALF_NITRATE)
    with_nitrite = (1.0 - with_oxygen - with_nitrate) * nitrite / (nitrite + HALF_NITRITE)
    with_sulfate = 1.0 - with_oxygen - with_nitrate - with_nitrite
    first_nitr = RATE_AMMONIUM * ammonium * with_oxygen
    second_nitr = RATE_NITRITE * nitrite * with_oxygen
    sulfide_ox = RATE_SULFIDE * sulfide * with_oxygen
    return jnp.stack(
        [
            -1.3 * breakdown * with_oxygen
            - 1.5 * first_nitr
            - 0.5 * second_nitr
            - 2.0 * sulfide_ox,
            -0.9 * breakdown * with_nitrate + second_nitr,
            0.9 * breakdown * with_nitrate
            - 0.6 * breakdown * with_nitrite
            + (1.0 - YIELD_NITROUS) * first_nitr
            - second_nitr,
            0.15 * breakdown - first_nitr,
            0.1 * breakdown,
            -breakdown,
            0.5 * breakdown * with_sulfate - sulfide_ox,
            YIELD_NITROUS * first_nitr - RATE_NITROUS * nitrous * (1.0 - with_oxygen),
        ]
    )


def body(
    surface_old,
    surface_forcing,
    surface_coeff,
    ocean_mask,
    column_depth,
    east_depth,
    tracers,
    u_clinic,
    v_clinic,
):
    mask_float = ocean_mask.astype(jnp.float32)
    right_side = surface_coeff * surface_old + surface_forcing
    surface = plain_solve(right_side, mask_float, surface_coeff)
    band_flow = -BARO_GAIN * (jnp.roll(surface, -1, axis=1) - surface)
    moved = lax.all_to_all(
        jnp.stack([surface, band_flow]), "lon", split_axis=2, concat_axis=1, tiled=True
    )
    strip_surface = moved[0].T
    east_baro = moved[1].T
    above_surface = jnp.concatenate([strip_surface[:, 1:], strip_surface[:, -1:]], axis=1)
    north_baro = -BARO_GAIN * (above_surface - strip_surface)
    wet, east_open, north_open, below_open, east_flow, north_flow = open_faces(
        column_depth, east_depth, east_baro, north_baro, u_clinic, v_clinic
    )
    masked = tracers * wet[None]
    tracer_count = masked.shape[0]
    columns_here = masked.shape[2]
    stacked = jnp.concatenate([masked, east_flow[None], east_open[None]], axis=0)
    padded = padded_2(stacked, (("lon", 2),), 2, True)
    tracer_pad = padded[:tracer_count]
    west_flow = padded[tracer_count, :, 1:2]
    west_open = padded[tracer_count + 1, :, 1:2]
    flow_all = jnp.concatenate([west_flow, east_flow], axis=1)
    open_all = jnp.concatenate([west_open, east_open], axis=1)
    center = tracer_pad[:, :, 1 : columns_here + 2]
    east_one = tracer_pad[:, :, 2 : columns_here + 3]
    west_one = tracer_pad[:, :, 0 : columns_here + 1]
    east_two = tracer_pad[:, :, 3 : columns_here + 4]
    face_east = (7.0 * (center + east_one) - (west_one + east_two)) / 12.0
    flux_all = flow_all[None] * face_east - HORIZ_DIFF * (east_one - center) * open_all[None]
    conv_east = flux_all[:, :, :-1] - flux_all[:, :, 1:]
    transport = conv_east + meridional_vertical(
        masked, north_flow[None], north_open[None], below_open[None]
    )
    tendency = transport + redox_sources(masked)
    tracers_new = tracers + wet[None] * tendency
    return (surface, tracers_new)


def solution(mesh):
    in_specs = (
        P(("member", "lon"), None),
        P(("member", "lon"), None),
        P("lon", None),
        P("lon", None),
        P("lon", None),
        P("lon", None),
        P("member", None, "lon", None),
        P("member", "lon", None),
        P("member", "lon", None),
    )
    out_specs = (P(("member", "lon"), None), P("member", None, "lon", None))
    return jax.shard_map(body, mesh=mesh, in_specs=in_specs, out_specs=out_specs, check_vma=False)
```

profile of v0, /device:TPU:1, one launch (start us, length us, event | category | flops | bytes accessed | tf_op | source)
XLA Modules:
  0.0 331.7 jit_solution(14252063561252996319)
XLA Ops:
  1.5 4.5 %collective-permute-start.1 = (f32[1,256]{1,0:T(1,128)S(1)}, f32[1,256]{1,0:T(1,128)S(1)}, u32[]{:S(2)}, u32[]{:S(2)}) collective-permute-start(f32[1,256]{1,0:T(1,128)S(1)} %get-tuple-element.59), channel_id=1, source_target_pairs={{0,1},{1,2},{2,3},{3,4},{4,5},{5,6},{6,7},{7,8},{8,9},{9,10},{10,1... | collective-permute-start | bytes 3080 | tf_op jit(solution)/shard_map/ppermute | solution.py:28
  8.8 4.9 %copy_multiply_fusion = f32[8,16,16,512]{3,1,2,0:T(8,128)S(1)} fusion(f32[8,16,16,512]{3,2,1,0:T(8,128)} %param.15, f32[16,16,512]{2,0,1:T(8,128)S(1)} %fusion.20), kind=kLoop, calls=%fused_computation.19 | loop fusion | flops 1048576 | bytes 8912896 | tf_op jit(solution)/shard_map/mul | solution.py:163
  19.1 30.3 %all-reduce.6 = (f32[]{:T(128)}, f32[]{:T(128)}) all-reduce(f32[]{:T(128)} %get-tuple-element.9, f32[]{:T(128)} %get-tuple-element.8), channel_id=1, replica_groups=mesh['member'=2,'lon'=16] {'lon'}, use_global_device_ids=true, to_apply=%region_1.0 | all-reduce | flops 2 | bytes 16 | tf_op jit(solution)/shard_map/psum | solution.py:51
  51.5 32.8 %psum.58 = f32[]{:T(128)} all-reduce(f32[]{:T(128)} %multiply_reduce_fusion.4), channel_id=1, replica_groups=mesh['member'=2,'lon'=16] {'lon'}, use_global_device_ids=true, to_apply=%region_5.6 | all-reduce | flops 1 | bytes 8 | tf_op jit(solution)/shard_map/psum | solution.py:51
  88.4 3.0 collective-permute-start.3
  92.8 29.0 %psum.59 = f32[]{:T(128)} all-reduce(f32[]{:T(128)} %get-tuple-element.20), channel_id=1, replica_groups=mesh['member'=2,'lon'=16] {'lon'}, use_global_device_ids=true, to_apply=%region_7.8 | all-reduce | flops 1 | bytes 8 | tf_op jit(solution)/shard_map/psum | solution.py:61
  123.7 31.1 %psum.60 = f32[]{:T(128)} all-reduce(f32[]{:T(128)} %get-tuple-element.18), channel_id=1, replica_groups=mesh['member'=2,'lon'=16] {'lon'}, use_global_device_ids=true, to_apply=%region_9.10 | all-reduce | flops 1 | bytes 8 | tf_op jit(solution)/shard_map/psum | solution.py:51
  156.2 2.5 collective-permute-start.4
  158.9 3.0 collective-permute-start.5
  163.3 29.0 %psum.61 = f32[]{:T(128)} all-reduce(f32[]{:T(128)} %get-tuple-element.14), channel_id=1, replica_groups=mesh['member'=2,'lon'=16] {'lon'}, use_global_device_ids=true, to_apply=%region_11.12 | all-reduce | flops 1 | bytes 8 | tf_op jit(solution)/shard_map/psum | solution.py:61
  194.2 31.1 %psum.62 = f32[]{:T(128)} all-reduce(f32[]{:T(128)} %multiply_reduce_fusion), channel_id=1, replica_groups=mesh['member'=2,'lon'=16] {'lon'}, use_global_device_ids=true, to_apply=%region_13.14 | all-reduce | flops 1 | bytes 8 | tf_op jit(solution)/shard_map/psum | solution.py:51
  226.8 2.5 collective-permute-start.6
  229.4 3.0 collective-permute-start.7
  233.8 5.0 %slice.315 = f32[8,15,16,512]{3,1,2,0:T(8,128)} slice(f32[8,16,16,512]{3,1,2,0:T(8,128)} %copy-done), slice={[0:8], [1:16], [0:16], [0:512]} | slice | bytes 7864320 | tf_op jit(solution)/shard_map/slice | solution.py:94
  238.9 29.0 %psum.63 = f32[]{:T(128)} all-reduce(f32[]{:T(128)} %fusion.29), channel_id=1, replica_groups=mesh['member'=2,'lon'=16] {'lon'}, use_global_device_ids=true, to_apply=%region_15.16 | all-reduce | flops 1 | bytes 8 | tf_op jit(solution)/shard_map/psum | solution.py:61
  270.6 4.9 %all-to-all-start = ((f32[16,1,1024]{2,1,0:T(1,128)}), f32[16,1,1024]{2,1,0:T(1,128)S(1)}, u32[]{:S(2)}, u32[]{:S(2)}) async-start(f32[16,1,1024]{2,1,0:T(1,128)} %reshape.32), calls=%async_computation | async-start | bytes 131072 | tf_op jit(solution)/shard_map/all_to_all | solution.py:153
  276.3 5.3 %all-to-all-done = f32[16,1,1024]{2,1,0:T(1,128)S(1)} async-done(((f32[16,1,1024]{2,1,0:T(1,128)}), f32[16,1,1024]{2,1,0:T(1,128)S(1)}, u32[]{:S(2)}, u32[]{:S(2)}) %all-to-all-start) | async-done | bytes 65568 | tf_op jit(solution)/shard_map/all_to_all | solution.py:153
  284.2 2.6 pad_maximum_fusion.3
  289.6 3.8 %fusion.6 = (f32[8,16,16,512]{3,1,2,0:T(8,128)S(1)}, f32[8,16,16,512]{3,1,2,0:T(8,128)S(1)}) fusion(f32[8,16,16,512]{3,1,2,0:T(8,128)S(1)} %copy-done.1, f32[16,16,512]{2,0,1:T(8,128)S(1)} %get-tuple-element.36, f32[16,16,512]{2,0,1:T(8,128)S(1)} %get-tuple-element.35, f32[16,16,512]{2,0,1:T(8,128)S(1)} %get-tuple-element.39, f32[8,15,16,512]{3,1,2,0:T(8,128)S(1)} %copy-done.2), kind=kLoop, calls=%fused_computation.12 | loop fusion | flops 10485760 | bytes 18087936 | tf_op jit(solution)/shard_map/sub | solution.py:90
  293.8 8.6 %collective-permute-done.8 = f32[10,16,2,512]{3,1,2,0:T(8,128)} collective-permute-done((f32[10,16,2,512]{3,1,2,0:T(8,128)}, f32[10,16,2,512]{3,1,2,0:T(8,128)}, u32[]{:S(2)}, u32[]{:S(2)}) %collective-permute-start.8) | collective-permute-done | bytes 655392 | tf_op jit(solution)/shard_map/ppermute | solution.py:28
  304.8 4.4 %maximum_maximum_fusion = (f32[10,16,18,512]{3,1,2,0:T(8,128)S(1)}, f32[10,16,18,512]{3,1,2,0:T(8,128)}) fusion(f32[1,16,16,512]{3,1,2,0:T(8,128)S(1)} %copy-done.6, f32[1,16,16,512]{3,1,2,0:T(8,128)S(1)} %fusion.64, f32[8,16,16,512]{3,1,2,0:T(8,128)S(1)} %copy-done.1, f32[10,16,2,512]{3,1,2,0:T(8,128)} %collective-permute-done.8, ...), kind=kLoop, calls=%fused_computation | loop fusion | flops 8847360 | bytes 18350080 | tf_op jit(solution)/shard_map/concatenate | solution.py:32
  309.2 6.3 %fusion.2 = f32[8,16,17,512]{3,1,2,0:T(8,128)} fusion(f32[10,16,18,512]{3,1,2,0:T(8,128)} %get-tuple-element.28, f32[10,16,18,512]{3,1,2,0:T(8,128)S(1)} %get-tuple-element.27, f32[16,17,512]{2,0,1:T(8,128)S(1)} %get-tuple-element.65, f32[16,17,512]{2,0,1:T(8,128)S(1)} %get-tuple-element.64), kind=kLoop, calls=%fused_computation.8 | loop fusion | flops 8912896 | bytes 23396352 | tf_op jit(solution)/shard_map/sub | solution.py:178
  315.5 11.7 %fusion.10 = f32[8,16,16,512]{3,1,2,0:T(8,128)S(1)} fusion(f32[8,16,16,512]{3,1,2,0:T(8,128)} %copy-done.4, f32[8,16,17,512]{3,1,2,0:T(8,128)} %fusion.2, f32[8,16,16,512]{3,1,2,0:T(8,128)S(1)} %get-tuple-element.32, f32[8,15,16,512]{3,1,2,0:T(8,128)S(1)} %bitcast.28, f32[8,16,16,512]{3,1,2,0:T(8,128)S(1)} %get-tuple-element.31, ...), kind=kLoop, calls=%fused_computation.17 | loop fusion | flops 8388608 | bytes 38002688 | tf_op jit(solution)/shard_map/add | solution.py:184
  327.2 4.5 %copy.35 = f32[8,16,16,512]{3,2,1,0:T(8,128)} copy(f32[8,16,16,512]{3,1,2,0:T(8,128)S(1)} %fusion.10) | data formatting | bytes 8388608
  (115 shorter events, 28.4 us)
Async XLA Ops:
  1.5 16.9 %collective-permute-start.1 = (f32[1,256]{1,0:T(1,128)S(1)}, f32[1,256]{1,0:T(1,128)S(1)}, u32[]{:S(2)}, u32[]{:S(2)}) collective-permute-start(f32[1,256]{1,0:T(1,128)S(1)} %get-tuple-element.59), channel_id=1, source_target_pairs={{0,1},{1,2},{2,3},{3,4},{4,5},{5,6},{6,7},{7,8},{8,9},{9,10},{10,1... | collective-permute-start | bytes 3080 | tf_op jit(solution)/shard_map/ppermute | solution.py:28
  6.0 12.3 %collective-permute-start = (f32[1,256]{1,0:T(1,128)S(1)}, f32[1,256]{1,0:T(1,128)S(1)}, u32[]{:S(2)}, u32[]{:S(2)}) collective-permute-start(f32[1,256]{1,0:T(1,128)S(1)} %get-tuple-element.58), channel_id=1, source_target_pairs={{1,0},{2,1},{3,2},{4,3},{5,4},{6,5},{7,6},{8,7},{9,8},{10,9},{11,1... | collective-permute-start | bytes 3080 | tf_op jit(solution)/shard_map/ppermute | solution.py:31
  8.8 185.3 %copy-start.3 = (f32[16,16,512]{2,0,1:T(8,128)}, f32[16,16,512]{2,0,1:T(8,128)S(1)}, u32[]{:S(2)}) copy-start(f32[16,16,512]{2,0,1:T(8,128)S(1)} %fusion.20) | copy-start | bytes 1572868
  15.1 2.9 copy-start.13
  15.1 3.2 copy-start.10
  15.1 3.2 copy-start.11
  18.0 266.1 %copy-start.5 = (f32[1,16,16,512]{3,1,2,0:T(8,128)}, f32[1,16,16,512]{3,1,2,0:T(8,128)S(1)}, u32[]{:S(2)}) copy-start(f32[1,16,16,512]{3,1,2,0:T(8,128)S(1)} %fusion.21) | copy-start | bytes 1572868
  85.7 5.8 %collective-permute-start.2 = (f32[1,256]{1,0:T(1,128)S(1)}, f32[1,256]{1,0:T(1,128)S(1)}, u32[]{:S(2)}, u32[]{:S(2)}) collective-permute-start(f32[1,256]{1,0:T(1,128)S(1)} %get-tuple-element.52), channel_id=1, source_target_pairs={{1,0},{2,1},{3,2},{4,3},{5,4},{6,5},{7,6},{8,7},{9,8},{10,9},{11,1... | collective-permute-start | bytes 3080 | tf_op jit(solution)/shard_map/ppermute | solution.py:31
  88.4 3.7 %collective-permute-start.3 = (f32[1,256]{1,0:T(1,128)S(1)}, f32[1,256]{1,0:T(1,128)S(1)}, u32[]{:S(2)}, u32[]{:S(2)}) collective-permute-start(f32[1,256]{1,0:T(1,128)S(1)} %get-tuple-element.53), channel_id=1, source_target_pairs={{0,1},{1,2},{2,3},{3,4},{4,5},{5,6},{6,7},{7,8},{8,9},{9,10},{10,1... | collective-permute-start | bytes 3080 | tf_op jit(solution)/shard_map/ppermute | solution.py:28
  156.2 5.8 %collective-permute-start.4 = (f32[1,256]{1,0:T(1,128)S(1)}, f32[1,256]{1,0:T(1,128)S(1)}, u32[]{:S(2)}, u32[]{:S(2)}) collective-permute-start(f32[1,256]{1,0:T(1,128)S(1)} %get-tuple-element.46), channel_id=1, source_target_pairs={{1,0},{2,1},{3,2},{4,3},{5,4},{6,5},{7,6},{8,7},{9,8},{10,9},{11,1... | collective-permute-start | bytes 3080 | tf_op jit(solution)/shard_map/ppermute | solution.py:31
  158.9 3.7 %collective-permute-start.5 = (f32[1,256]{1,0:T(1,128)S(1)}, f32[1,256]{1,0:T(1,128)S(1)}, u32[]{:S(2)}, u32[]{:S(2)}) collective-permute-start(f32[1,256]{1,0:T(1,128)S(1)} %get-tuple-element.47), channel_id=1, source_target_pairs={{0,1},{1,2},{2,3},{3,4},{4,5},{5,6},{6,7},{7,8},{8,9},{9,10},{10,1... | collective-permute-start | bytes 3080 | tf_op jit(solution)/shard_map/ppermute | solution.py:28
  226.8 5.8 %collective-permute-start.6 = (f32[1,256]{1,0:T(1,128)S(1)}, f32[1,256]{1,0:T(1,128)S(1)}, u32[]{:S(2)}, u32[]{:S(2)}) collective-permute-start(f32[1,256]{1,0:T(1,128)S(1)} %get-tuple-element.44), channel_id=1, source_target_pairs={{1,0},{2,1},{3,2},{4,3},{5,4},{6,5},{7,6},{8,7},{9,8},{10,9},{11,1... | collective-permute-start | bytes 3080 | tf_op jit(solution)/shard_map/ppermute | solution.py:31
  229.4 3.7 %collective-permute-start.7 = (f32[1,256]{1,0:T(1,128)S(1)}, f32[1,256]{1,0:T(1,128)S(1)}, u32[]{:S(2)}, u32[]{:S(2)}) collective-permute-start(f32[1,256]{1,0:T(1,128)S(1)} %get-tuple-element.45), channel_id=1, source_target_pairs={{0,1},{1,2},{2,3},{3,4},{4,5},{5,6},{6,7},{7,8},{8,9},{9,10},{10,1... | collective-permute-start | bytes 3080 | tf_op jit(solution)/shard_map/ppermute | solution.py:28
  238.9 44.9 %copy-start.8 = (f32[16,16,512]{2,1,0:T(8,128)S(1)}, f32[16,16,512]{2,1,0:T(8,128)}, u32[]{:S(2)}) copy-start(f32[16,16,512]{2,1,0:T(8,128)} %param.16) | copy-start | bytes 1572868
  269.3 17.5 %copy-start.12 = (f32[32,256]{1,0:T(8,128)}, f32[32,256]{1,0:T(8,128)S(1)}, u32[]{:S(2)}) copy-start(f32[32,256]{1,0:T(8,128)S(1)} %multiply_add_fusion) | copy-start | bytes 98308
  270.6 11.0 %all-to-all-start = ((f32[16,1,1024]{2,1,0:T(1,128)}), f32[16,1,1024]{2,1,0:T(1,128)S(1)}, u32[]{:S(2)}, u32[]{:S(2)}) async-start(f32[16,1,1024]{2,1,0:T(1,128)} %reshape.32), calls=%async_computation | async-start | bytes 131072 | tf_op jit(solution)/shard_map/all_to_all | solution.py:153
  283.4 4.6 %copy-start.14 = (s32[16,512]{1,0:T(8,128)S(1)}, s32[16,512]{1,0:T(8,128)}, u32[]{:S(2)}) copy-start(s32[16,512]{1,0:T(8,128)} %param.13) | copy-start | bytes 98308
  284.2 5.4 %copy-start.1 = (f32[8,16,16,512]{3,1,2,0:T(8,128)S(1)}, f32[8,16,16,512]{3,1,2,0:T(8,128)}, u32[]{:S(2)}) copy-start(f32[8,16,16,512]{3,1,2,0:T(8,128)} %copy-done) | copy-start | bytes 12582916
  284.2 5.4 %copy-start.2 = (f32[8,15,16,512]{3,1,2,0:T(8,128)S(1)}, f32[8,15,16,512]{3,1,2,0:T(8,128)}, u32[]{:S(2)}) copy-start(f32[8,15,16,512]{3,1,2,0:T(8,128)} %slice.315) | copy-start | bytes 11796484
  286.8 15.5 %collective-permute-start.8 = (f32[10,16,2,512]{3,1,2,0:T(8,128)}, f32[10,16,2,512]{3,1,2,0:T(8,128)}, u32[]{:S(2)}, u32[]{:S(2)}) collective-permute-start(f32[10,16,2,512]{3,1,2,0:T(8,128)} %get-tuple-element.29), channel_id=1, source_target_pairs={{0,1},{1,2},{2,3},{3,4},{4,5},{5,6},{6,7},{7,8},{8,9},{9,10},{10,1... | collective-permute-start | bytes 1966088 | tf_op jit(solution)/shard_map/ppermute | solution.py:28
  287.5 17.3 %collective-permute-start.9 = (f32[10,16,2,512]{3,1,2,0:T(8,128)}, f32[10,16,2,512]{3,1,2,0:T(8,128)}, u32[]{:S(2)}, u32[]{:S(2)}) collective-permute-start(f32[10,16,2,512]{3,1,2,0:T(8,128)} %get-tuple-element.30), channel_id=1, source_target_pairs={{1,0},{2,1},{3,2},{4,3},{5,4},{6,5},{7,6},{8,7},{9,8},{10,9},{11,1... | collective-permute-start | bytes 1966088 | tf_op jit(solution)/shard_map/ppermute | solution.py:31
  289.6 3.8 %copy-start.9 = (f32[16,16,512]{2,1,0:T(8,128)S(1)}, f32[16,16,512]{2,1,0:T(8,128)}, u32[]{:S(2)}) copy-start(f32[16,16,512]{2,1,0:T(8,128)} %param.16) | copy-start | bytes 1572868
  289.6 13.5 %copy-start.7 = (f32[16,16,512]{2,0,1:T(8,128)S(1)}, f32[16,16,512]{2,0,1:T(8,128)}, u32[]{:S(2)}) copy-start(f32[16,16,512]{2,0,1:T(8,128)} %fusion.19) | copy-start | bytes 1572868
  289.6 15.2 %copy-start.6 = (f32[1,16,16,512]{3,1,2,0:T(8,128)S(1)}, f32[1,16,16,512]{3,1,2,0:T(8,128)}, u32[]{:S(2)}) copy-start(f32[1,16,16,512]{3,1,2,0:T(8,128)} %copy-done.5) | copy-start | bytes 1572868
  (2 other events, 4.0 us)
where the time goes:
time: 333 us; the launch traced here: 332 us
  blocking collectives  212 us (64%)
  other arithmetic  46.5 us (14%)
  starting transfers between devices  29.1 us (9%)
  waiting for transfers between devices  16.8 us (5%)
  local copies, waits for them, and re-layouts  16.6 us (5%)
  between operations  10.4 us (3%)
    psum x4, blocking collectives, squared_total(): return lax.psum(jnp.sum(residual * residual), 'lon')  125 us
    psum x3, blocking collectives, plain_solve(): curvature = lax.psum(jnp.sum(direction * applied), 'lon')  87 us
    ppermute x5, starting transfers between devices, padded_2(): lax.ppermute(lax.slice_in_dim(block, block.shape[dim] - width, None, axis...  14.2 us
    add x1, other arithmetic, body(): tracers_new = tracers + wet[None] * tendency  11.7 us
    ppermute x5, starting transfers between devices, padded_2(): lax.ppermute(lax.slice_in_dim(block, 0, width, axis=dim), axis, backward)  10 us
    ppermute x5, waiting for transfers between devices, padded_2(): lax.ppermute(lax.slice_in_dim(block, block.shape[dim] - width, None, axis...  10 us
    unnamed x33, local copies, waits for them, and re-layouts  7.77 us
  transfers between devices with their start and end apart: 11, of which 6 were waited for; matrix products, arithmetic and copies ran while one was open for 5% of the time, Pallas kernels for 0%

commit v1 on v0

--- a/solution.py
+++ b/solution.py
@@ -16,6 +16,17 @@
 HALF_NITRATE = 0.3
 HALF_NITRITE = 0.3
 YIELD_NITROUS = 0.3
+
+
+def in_blocks(x, dim, length):
+    before, after = (x.shape[:dim], x.shape[dim + 1 :])
+    return jnp.moveaxis(x.reshape(*before, length, -1, *after), dim, 0)
+
+
+def joined_along(blocks, dim):
+    blocks = jnp.moveaxis(blocks, 0, dim)
+    lengths = blocks.shape
+    return blocks.reshape(*lengths[:dim], lengths[dim] * lengths[dim + 1], *lengths[dim + 2 :])
 
 
 def padded_2(block, sides, width, periodic):
@@ -150,9 +161,16 @@
     right_side = surface_coeff * surface_old + surface_forcing
     surface = plain_solve(right_side, mask_float, surface_coeff)
     band_flow = -BARO_GAIN * (jnp.roll(surface, -1, axis=1) - surface)
-    moved = lax.all_to_all(
-        jnp.stack([surface, band_flow]), "lon", split_axis=2, concat_axis=1, tiled=True
-    )
+    x = jnp.stack([surface, band_flow])
+    peers, place = (lax.axis_size("lon"), lax.axis_index("lon"))
+    tiles = in_blocks(x, 2, peers)
+    whole = tiles
+    for step in range(1, peers):
+        target_2, source_2 = ((place + step) % peers, (place - step) % peers)
+        sent = lax.dynamic_index_in_dim(tiles, target_2, 0)
+        other = lax.ppermute(sent, "lon", [(i_2, (i_2 + step) % peers) for i_2 in range(peers)])
+        whole = lax.dynamic_update_slice_in_dim(whole, other, source_2, axis=0)
+    moved = joined_along(whole, 1)
     strip_surface = moved[0].T
     east_baro = moved[1].T
     above_surface = jnp.concatenate([strip_surface[:, 1:], strip_surface[:, -1:]], axis=1)

time: 333 us -> 357 us (1.072)
  starting transfers between devices: 29.1 us -> 44.9 us
  other arithmetic: 46.5 us -> 53.9 us
    ppermute x0 -> x15, starting transfers between devices: none -> 20.6 us  [body(): lax.ppermute(sent, 'lon', [(i_2, (i_2 + step) % peers) for i_2 in range(p...]
    unnamed x7, other arithmetic: 1.76 us -> 7.59 us
    all_to_all x1 -> x0, waiting for transfers between devices: 5.26 us -> none  [body(): lax.all_to_all(jnp.stack([surface, band_flow]), 'lon', split_axis=2, conc...]
    all_to_all x1 -> x0, starting transfers between devices: 4.92 us -> none  [body(): lax.all_to_all(jnp.stack([surface, band_flow]), 'lon', split_axis=2, conc...]
    unnamed x33 -> x26, local copies, waits for them, and re-layouts: 7.77 us -> 8.65 us
  transfers between devices with their start and end apart: 11 -> 25, of which waited for: 6 -> 9; matrix products, arithmetic and copies ran while one was open for 5% -> 8% of each run, Pallas kernels for 0% -> 0%
where the time goes in v1:
time: 357 us; the launch traced here: 356 us
  blocking collectives  213 us (60%)
  other arithmetic  53.9 us (15%)
  starting transfers between devices  44.9 us (13%)
  waiting for transfers between devices  17.8 us (5%)
  local copies, waits for them, and re-layouts  15.8 us (4%)
  between operations  11.1 us (3%)
    psum x4, blocking collectives, squared_total(): return lax.psum(jnp.sum(residual * residual), 'lon')  127 us
    psum x3, blocking collectives, plain_solve(): curvature = lax.psum(jnp.sum(direction * applied), 'lon')  85.2 us
    ppermute x15, starting transfers between devices, body(): lax.ppermute(sent, 'lon', [(i_2, (i_2 + step) % peers) for i_2 in range(p...  20.6 us
    ppermute x5, starting transfers between devices, padded_2(): lax.ppermute(lax.slice_in_dim(block, block.shape[dim] - width, None, axis...  14.6 us
    add x1, other arithmetic, body(): tracers_new = tracers + wet[None] * tendency  11.8 us
    ppermute x5, waiting for transfers between devices, padded_2(): lax.ppermute(lax.slice_in_dim(block, block.shape[dim] - width, None, axis...  11.6 us
    ppermute x5, starting transfers between devices, padded_2(): lax.ppermute(lax.slice_in_dim(block, 0, width, axis=dim), axis, backward)  9.59 us
    unnamed x26, local copies, waits for them, and re-layouts  8.65 us
  transfers between devices with their start and end apart: 25, of which 9 were waited for; matrix products, arithmetic and copies ran while one was open for 8% of the time, Pallas kernels for 0%

profile of v1, /device:TPU:1, one launch (start us, length us, event | category | flops | bytes accessed | tf_op | source)
XLA Modules:
  0.0 356.0 jit_solution(4395960839789148151)
XLA Ops:
  4.2 4.5 %collective-permute-start.1 = (f32[1,256]{0,1:T(8,128)S(1)}, f32[1,256]{0,1:T(8,128)S(1)}, u32[]{:S(2)}, u32[]{:S(2)}) collective-permute-start(f32[1,256]{0,1:T(8,128)S(1)} %get-tuple-element.75), channel_id=1, source_target_pairs={{0,1},{1,2},{2,3},{3,4},{4,5},{5,6},{6,7},{7,8},{8,9},{9,10},{10,1... | collective-permute-start | bytes 3080 | tf_op jit(solution)/shard_map/ppermute | solution.py:39
  13.5 4.7 %copy_multiply_fusion = f32[8,16,16,512]{3,1,2,0:T(8,128)S(1)} fusion(f32[8,16,16,512]{3,2,1,0:T(8,128)} %param.15, f32[16,16,512]{2,0,1:T(8,128)S(1)} %fusion.20), kind=kLoop, calls=%fused_computation.19 | loop fusion | flops 1048576 | bytes 8912896 | tf_op jit(solution)/shard_map/mul | solution.py:181
  19.7 2.9 slice.315
  30.6 30.3 %all-reduce.6 = (f32[]{:T(128)}, f32[]{:T(128)}) all-reduce(f32[]{:T(128)} %get-tuple-element.11, f32[]{:T(128)} %get-tuple-element.10), channel_id=1, replica_groups=mesh['member'=2,'lon'=16] {'lon'}, use_global_device_ids=true, to_apply=%region_1.0 | all-reduce | flops 2 | bytes 16 | tf_op jit(solution)/shard_map/psum | solution.py:62
  62.7 32.8 %psum.58 = f32[]{:T(128)} all-reduce(f32[]{:T(128)} %multiply_reduce_fusion.4), channel_id=1, replica_groups=mesh['member'=2,'lon'=16] {'lon'}, use_global_device_ids=true, to_apply=%region_5.6 | all-reduce | flops 1 | bytes 8 | tf_op jit(solution)/shard_map/psum | solution.py:62
  97.0 2.6 collective-permute-start.2
  99.5 3.0 collective-permute-start.3
  105.3 27.9 %psum.59 = f32[]{:T(128)} all-reduce(f32[]{:T(128)} %get-tuple-element.22), channel_id=1, replica_groups=mesh['member'=2,'lon'=16] {'lon'}, use_global_device_ids=true, to_apply=%region_7.8 | all-reduce | flops 1 | bytes 8 | tf_op jit(solution)/shard_map/psum | solution.py:72
  135.1 32.2 %psum.60 = f32[]{:T(128)} all-reduce(f32[]{:T(128)} %get-tuple-element.20), channel_id=1, replica_groups=mesh['member'=2,'lon'=16] {'lon'}, use_global_device_ids=true, to_apply=%region_9.10 | all-reduce | flops 1 | bytes 8 | tf_op jit(solution)/shard_map/psum | solution.py:62
  171.5 3.0 collective-permute-start.5
  178.1 28.0 %psum.61 = f32[]{:T(128)} all-reduce(f32[]{:T(128)} %get-tuple-element.16), channel_id=1, replica_groups=mesh['member'=2,'lon'=16] {'lon'}, use_global_device_ids=true, to_apply=%region_11.12 | all-reduce | flops 1 | bytes 8 | tf_op jit(solution)/shard_map/psum | solution.py:72
  208.1 32.0 %psum.62 = f32[]{:T(128)} all-reduce(f32[]{:T(128)} %multiply_reduce_fusion), channel_id=1, replica_groups=mesh['member'=2,'lon'=16] {'lon'}, use_global_device_ids=true, to_apply=%region_13.14 | all-reduce | flops 1 | bytes 8 | tf_op jit(solution)/shard_map/psum | solution.py:62
  242.4 2.6 collective-permute-start.6
  245.0 3.0 collective-permute-start.7
  252.0 29.3 %psum.63 = f32[]{:T(128)} all-reduce(f32[]{:T(128)} %fusion.30), channel_id=1, replica_groups=mesh['member'=2,'lon'=16] {'lon'}, use_global_device_ids=true, to_apply=%region_15.16 | all-reduce | flops 1 | bytes 8 | tf_op jit(solution)/shard_map/psum | solution.py:72
  283.7 7.6 %collective-permute-start.12 = (f32[1,2,32,16]{2,3,0,1:T(8,128)S(1)}, f32[1,2,32,16]{2,3,0,1:T(8,128)S(1)}, u32[]{:S(2)}, u32[]{:S(2)}) collective-permute-start(f32[1,2,32,16]{2,3,0,1:T(8,128)S(1)} %get-tuple-element.46), channel_id=1, source_target_pairs={{0,5},{1,6},{2,7},{3,8},{4,9},{5,10},{6,11},{7,12},{8,13},{9,14},{... | collective-permute-start | bytes 12296 | tf_op jit(solution)/shard_map/ppermute | solution.py:171
  300.7 2.6 collective-permute-start.20
  308.3 2.6 pad_maximum_fusion.4
  313.8 3.8 %fusion.6 = (f32[8,16,16,512]{3,1,2,0:T(8,128)S(1)}, f32[8,16,16,512]{3,1,2,0:T(8,128)S(1)}) fusion(f32[8,16,16,512]{3,1,2,0:T(8,128)S(1)} %copy-done.1, f32[16,16,512]{2,0,1:T(8,128)S(1)} %get-tuple-element.38, f32[16,16,512]{2,0,1:T(8,128)S(1)} %get-tuple-element.37, f32[16,16,512]{2,0,1:T(8,128)S(1)} %get-tuple-element.80, f32[8,15,16,512]{3,1,2,0:T(8,128)S(1)} %copy-done.2), kind=kLoop, calls=%fused_computation.12 | loop fusion | flops 10485760 | bytes 18087936 | tf_op jit(solution)/shard_map/sub | solution.py:101
  318.0 8.9 %collective-permute-done.23 = f32[10,16,2,512]{3,1,2,0:T(8,128)S(1)} collective-permute-done((f32[10,16,2,512]{3,1,2,0:T(8,128)}, f32[10,16,2,512]{3,1,2,0:T(8,128)S(1)}, u32[]{:S(2)}, u32[]{:S(2)}) %collective-permute-start.23) | collective-permute-done | bytes 655392 | tf_op jit(solution)/shard_map/ppermute | solution.py:39
  329.1 4.3 %maximum_maximum_fusion = (f32[10,16,18,512]{3,1,2,0:T(8,128)S(1)}, f32[10,16,18,512]{3,1,2,0:T(8,128)}) fusion(f32[1,16,16,512]{3,1,2,0:T(8,128)S(1)} %copy-done.5, f32[1,16,16,512]{3,1,2,0:T(8,128)S(1)} %fusion.94, f32[8,16,16,512]{3,1,2,0:T(8,128)S(1)} %copy-done.1, f32[10,16,2,512]{3,1,2,0:T(8,128)S(1)} %collective-permute-done.23, ...), kind=kLoop, calls=%fused_computation | loop fusion | flops 8847360 | bytes 18350080 | tf_op jit(solution)/shard_map/concatenate | solution.py:43
  333.4 6.3 %fusion.2 = f32[8,16,17,512]{3,1,2,0:T(8,128)} fusion(f32[10,16,18,512]{3,1,2,0:T(8,128)} %get-tuple-element.30, f32[10,16,18,512]{3,1,2,0:T(8,128)S(1)} %get-tuple-element.29, f32[16,17,512]{2,0,1:T(8,128)S(1)} %get-tuple-element.82, f32[16,17,512]{2,0,1:T(8,128)S(1)} %get-tuple-element.81), kind=kLoop, calls=%fused_computation.8 | loop fusion | flops 8912896 | bytes 23396352 | tf_op jit(solution)/shard_map/sub | solution.py:196
  339.7 11.8 %fusion.10 = f32[8,16,16,512]{3,1,2,0:T(8,128)S(1)} fusion(f32[8,16,16,512]{3,1,2,0:T(8,128)} %fusion.13, f32[8,16,17,512]{3,1,2,0:T(8,128)} %fusion.2, f32[8,16,16,512]{3,1,2,0:T(8,128)S(1)} %get-tuple-element.34, f32[8,15,16,512]{3,1,2,0:T(8,128)S(1)} %bitcast.55, f32[8,16,16,512]{3,1,2,0:T(8,128)S(1)} %get-tuple-element.33, ...), kind=kLoop, calls=%fused_computation.17 | loop fusion | flops 8388608 | bytes 38002688 | tf_op jit(solution)/shard_map/add | solution.py:202
  351.5 4.5 %copy.103 = f32[8,16,16,512]{3,2,1,0:T(8,128)} copy(f32[8,16,16,512]{3,1,2,0:T(8,128)S(1)} %fusion.10) | data formatting | bytes 8388608
  (150 shorter events, 53.9 us)
Async XLA Ops:
  4.2 25.5 %collective-permute-start.1 = (f32[1,256]{0,1:T(8,128)S(1)}, f32[1,256]{0,1:T(8,128)S(1)}, u32[]{:S(2)}, u32[]{:S(2)}) collective-permute-start(f32[1,256]{0,1:T(8,128)S(1)} %get-tuple-element.75), channel_id=1, source_target_pairs={{0,1},{1,2},{2,3},{3,4},{4,5},{5,6},{6,7},{7,8},{8,9},{9,10},{10,1... | collective-permute-start | bytes 3080 | tf_op jit(solution)/shard_map/ppermute | solution.py:39
  8.8 20.9 %collective-permute-start = (f32[1,256]{0,1:T(8,128)S(1)}, f32[1,256]{0,1:T(8,128)S(1)}, u32[]{:S(2)}, u32[]{:S(2)}) collective-permute-start(f32[1,256]{0,1:T(8,128)S(1)} %get-tuple-element.74), channel_id=1, source_target_pairs={{1,0},{2,1},{3,2},{4,3},{5,4},{6,5},{7,6},{8,7},{9,8},{10,9},{11,1... | collective-permute-start | bytes 3080 | tf_op jit(solution)/shard_map/ppermute | solution.py:42
  97.0 6.3 %collective-permute-start.2 = (f32[1,256]{0,1:T(8,128)S(1)}, f32[1,256]{0,1:T(8,128)S(1)}, u32[]{:S(2)}, u32[]{:S(2)}) collective-permute-start(f32[1,256]{0,1:T(8,128)S(1)} %get-tuple-element.68), channel_id=1, source_target_pairs={{1,0},{2,1},{3,2},{4,3},{5,4},{6,5},{7,6},{8,7},{9,8},{10,9},{11,1... | collective-permute-start | bytes 3080 | tf_op jit(solution)/shard_map/ppermute | solution.py:42
  99.5 4.9 %collective-permute-start.3 = (f32[1,256]{0,1:T(8,128)S(1)}, f32[1,256]{0,1:T(8,128)S(1)}, u32[]{:S(2)}, u32[]{:S(2)}) collective-permute-start(f32[1,256]{0,1:T(8,128)S(1)} %get-tuple-element.69), channel_id=1, source_target_pairs={{0,1},{1,2},{2,3},{3,4},{4,5},{5,6},{6,7},{7,8},{8,9},{9,10},{10,1... | collective-permute-start | bytes 3080 | tf_op jit(solution)/shard_map/ppermute | solution.py:39
  168.9 6.3 %collective-permute-start.4 = (f32[1,256]{0,1:T(8,128)S(1)}, f32[1,256]{0,1:T(8,128)S(1)}, u32[]{:S(2)}, u32[]{:S(2)}) collective-permute-start(f32[1,256]{0,1:T(8,128)S(1)} %get-tuple-element.62), channel_id=1, source_target_pairs={{1,0},{2,1},{3,2},{4,3},{5,4},{6,5},{7,6},{8,7},{9,8},{10,9},{11,1... | collective-permute-start | bytes 3080 | tf_op jit(solution)/shard_map/ppermute | solution.py:42
  171.5 4.9 %collective-permute-start.5 = (f32[1,256]{0,1:T(8,128)S(1)}, f32[1,256]{0,1:T(8,128)}, u32[]{:S(2)}, u32[]{:S(2)}) collective-permute-start(f32[1,256]{0,1:T(8,128)S(1)} %get-tuple-element.63), channel_id=1, source_target_pairs={{0,1},{1,2},{2,3},{3,4},{4,5},{5,6},{6,7},{7,8},{8,9},{9,10},{10,1... | collective-permute-start | bytes 3080 | tf_op jit(solution)/shard_map/ppermute | solution.py:39
  242.4 6.6 %collective-permute-start.6 = (f32[1,256]{0,1:T(8,128)}, f32[1,256]{0,1:T(8,128)}, u32[]{:S(2)}, u32[]{:S(2)}) collective-permute-start(f32[1,256]{0,1:T(8,128)} %get-tuple-element.60), channel_id=1, source_target_pairs={{1,0},{2,1},{3,2},{4,3},{5,4},{6,5},{7,6},{8,7},{9,8},{10,9},{11,1... | collective-permute-start | bytes 3080 | tf_op jit(solution)/shard_map/ppermute | solution.py:42
  245.0 5.3 %collective-permute-start.7 = (f32[1,256]{0,1:T(8,128)}, f32[1,256]{0,1:T(8,128)}, u32[]{:S(2)}, u32[]{:S(2)}) collective-permute-start(f32[1,256]{0,1:T(8,128)} %get-tuple-element.61), channel_id=1, source_target_pairs={{0,1},{1,2},{2,3},{3,4},{4,5},{5,6},{6,7},{7,8},{8,9},{9,10},{10,1... | collective-permute-start | bytes 3080 | tf_op jit(solution)/shard_map/ppermute | solution.py:39
  283.4 7.8 %collective-permute-start.8 = (f32[1,2,32,16]{2,3,0,1:T(8,128)S(1)}, f32[1,2,32,16]{2,3,0,1:T(8,128)S(1)}, u32[]{:S(2)}, u32[]{:S(2)}) collective-permute-start(f32[1,2,32,16]{2,3,0,1:T(8,128)S(1)} %get-tuple-element.42), channel_id=1, source_target_pairs={{0,1},{1,2},{2,3},{3,4},{4,5},{5,6},{6,7},{7,8},{8,9},{9,10},{10,1... | collective-permute-start | bytes 12296 | tf_op jit(solution)/shard_map/ppermute | solution.py:171
  283.5 7.9 %collective-permute-start.9 = (f32[1,2,32,16]{2,3,0,1:T(8,128)S(1)}, f32[1,2,32,16]{2,3,0,1:T(8,128)S(1)}, u32[]{:S(2)}, u32[]{:S(2)}) collective-permute-start(f32[1,2,32,16]{2,3,0,1:T(8,128)S(1)} %get-tuple-element.43), channel_id=1, source_target_pairs={{0,2},{1,3},{2,4},{3,5},{4,6},{5,7},{6,8},{7,9},{8,10},{9,11},{10,... | collective-permute-start | bytes 12296 | tf_op jit(solution)/shard_map/ppermute | solution.py:171
  283.6 7.9 %collective-permute-start.10 = (f32[1,2,32,16]{2,3,0,1:T(8,128)S(1)}, f32[1,2,32,16]{2,3,0,1:T(8,128)S(1)}, u32[]{:S(2)}, u32[]{:S(2)}) collective-permute-start(f32[1,2,32,16]{2,3,0,1:T(8,128)S(1)} %get-tuple-element.44), channel_id=1, source_target_pairs={{0,3},{1,4},{2,5},{3,6},{4,7},{5,8},{6,9},{7,10},{8,11},{9,12},{10... | collective-permute-start | bytes 12296 | tf_op jit(solution)/shard_map/ppermute | solution.py:171
  283.6 10.4 %collective-permute-start.11 = (f32[1,2,32,16]{2,3,0,1:T(8,128)S(1)}, f32[1,2,32,16]{2,3,0,1:T(8,128)S(1)}, u32[]{:S(2)}, u32[]{:S(2)}) collective-permute-start(f32[1,2,32,16]{2,3,0,1:T(8,128)S(1)} %get-tuple-element.45), channel_id=1, source_target_pairs={{0,4},{1,5},{2,6},{3,7},{4,8},{5,9},{6,10},{7,11},{8,12},{9,13},{1... | collective-permute-start | bytes 12296 | tf_op jit(solution)/shard_map/ppermute | solution.py:171
  283.7 11.4 %collective-permute-start.12 = (f32[1,2,32,16]{2,3,0,1:T(8,128)S(1)}, f32[1,2,32,16]{2,3,0,1:T(8,128)S(1)}, u32[]{:S(2)}, u32[]{:S(2)}) collective-permute-start(f32[1,2,32,16]{2,3,0,1:T(8,128)S(1)} %get-tuple-element.46), channel_id=1, source_target_pairs={{0,5},{1,6},{2,7},{3,8},{4,9},{5,10},{6,11},{7,12},{8,13},{9,14},{... | collective-permute-start | bytes 12296 | tf_op jit(solution)/shard_map/ppermute | solution.py:171
  291.3 6.1 %collective-permute-start.13 = (f32[1,2,32,16]{2,3,0,1:T(8,128)S(1)}, f32[1,2,32,16]{2,3,0,1:T(8,128)S(1)}, u32[]{:S(2)}, u32[]{:S(2)}) collective-permute-start(f32[1,2,32,16]{2,3,0,1:T(8,128)S(1)} %get-tuple-element.48), channel_id=1, source_target_pairs={{0,6},{1,7},{2,8},{3,9},{4,10},{5,11},{6,12},{7,13},{8,14},{9,15},... | collective-permute-start | bytes 12296 | tf_op jit(solution)/shard_map/ppermute | solution.py:171
  291.4 7.4 %collective-permute-start.14 = (f32[1,2,32,16]{2,3,0,1:T(8,128)S(1)}, f32[1,2,32,16]{2,3,0,1:T(8,128)S(1)}, u32[]{:S(2)}, u32[]{:S(2)}) collective-permute-start(f32[1,2,32,16]{2,3,0,1:T(8,128)S(1)} %get-tuple-element.49), channel_id=1, source_target_pairs={{0,7},{1,8},{2,9},{3,10},{4,11},{5,12},{6,13},{7,14},{8,15},{9,0},... | collective-permute-start | bytes 12296 | tf_op jit(solution)/shard_map/ppermute | solution.py:171
  291.5 9.2 %collective-permute-start.15 = (f32[1,2,32,16]{2,3,0,1:T(8,128)S(1)}, f32[1,2,32,16]{2,3,0,1:T(8,128)S(1)}, u32[]{:S(2)}, u32[]{:S(2)}) collective-permute-start(f32[1,2,32,16]{2,3,0,1:T(8,128)S(1)} %get-tuple-element.50), channel_id=1, source_target_pairs={{0,8},{1,9},{2,10},{3,11},{4,12},{5,13},{6,14},{7,15},{8,0},{9,1},... | collective-permute-start | bytes 12296 | tf_op jit(solution)/shard_map/ppermute | solution.py:171
  294.0 9.3 %collective-permute-start.16 = (f32[1,2,32,16]{2,3,0,1:T(8,128)S(1)}, f32[1,2,32,16]{2,3,0,1:T(8,128)S(1)}, u32[]{:S(2)}, u32[]{:S(2)}) collective-permute-start(f32[1,2,32,16]{2,3,0,1:T(8,128)S(1)} %get-tuple-element.51), channel_id=1, source_target_pairs={{0,9},{1,10},{2,11},{3,12},{4,13},{5,14},{6,15},{7,0},{8,1},{9,2},... | collective-permute-start | bytes 12296 | tf_op jit(solution)/shard_map/ppermute | solution.py:171
  295.1 9.2 %collective-permute-start.17 = (f32[1,2,32,16]{2,3,0,1:T(8,128)S(1)}, f32[1,2,32,16]{2,3,0,1:T(8,128)S(1)}, u32[]{:S(2)}, u32[]{:S(2)}) collective-permute-start(f32[1,2,32,16]{2,3,0,1:T(8,128)S(1)} %get-tuple-element.52), channel_id=1, source_target_pairs={{0,10},{1,11},{2,12},{3,13},{4,14},{5,15},{6,0},{7,1},{8,2},{9,3},... | collective-permute-start | bytes 12296 | tf_op jit(solution)/shard_map/ppermute | solution.py:171
  297.4 6.9 %collective-permute-start.18 = (f32[1,2,32,16]{2,3,0,1:T(8,128)S(1)}, f32[1,2,32,16]{2,3,0,1:T(8,128)S(1)}, u32[]{:S(2)}, u32[]{:S(2)}) collective-permute-start(f32[1,2,32,16]{2,3,0,1:T(8,128)S(1)} %get-tuple-element.54), channel_id=1, source_target_pairs={{0,11},{1,12},{2,13},{3,14},{4,15},{5,0},{6,1},{7,2},{8,3},{9,4},{... | collective-permute-start | bytes 12296 | tf_op jit(solution)/shard_map/ppermute | solution.py:171
  298.8 5.6 %collective-permute-start.19 = (f32[1,2,32,16]{2,3,0,1:T(8,128)S(1)}, f32[1,2,32,16]{2,3,0,1:T(8,128)S(1)}, u32[]{:S(2)}, u32[]{:S(2)}) collective-permute-start(f32[1,2,32,16]{2,3,0,1:T(8,128)S(1)} %get-tuple-element.55), channel_id=1, source_target_pairs={{0,12},{1,13},{2,14},{3,15},{4,0},{5,1},{6,2},{7,3},{8,4},{9,5},{1... | collective-permute-start | bytes 12296 | tf_op jit(solution)/shard_map/ppermute | solution.py:171
  300.7 3.7 %collective-permute-start.20 = (f32[1,2,32,16]{2,3,0,1:T(8,128)S(1)}, f32[1,2,32,16]{2,3,0,1:T(8,128)S(1)}, u32[]{:S(2)}, u32[]{:S(2)}) collective-permute-start(f32[1,2,32,16]{2,3,0,1:T(8,128)S(1)} %get-tuple-element.53), channel_id=1, source_target_pairs={{0,13},{1,14},{2,15},{3,0},{4,1},{5,2},{6,3},{7,4},{8,5},{9,6},{10... | collective-permute-start | bytes 12296 | tf_op jit(solution)/shard_map/ppermute | solution.py:171
  304.3 3.2 collective-permute-start.22
  310.9 15.9 %collective-permute-start.23 = (f32[10,16,2,512]{3,1,2,0:T(8,128)}, f32[10,16,2,512]{3,1,2,0:T(8,128)S(1)}, u32[]{:S(2)}, u32[]{:S(2)}) collective-permute-start(f32[10,16,2,512]{3,1,2,0:T(8,128)} %get-tuple-element.31), channel_id=1, source_target_pairs={{0,1},{1,2},{2,3},{3,4},{4,5},{5,6},{6,7},{7,8},{8,9},{9,10},{10,1... | collective-permute-start | bytes 1966088 | tf_op jit(solution)/shard_map/ppermute | solution.py:39
  312.0 17.1 %collective-permute-start.24 = (f32[10,16,2,512]{3,1,2,0:T(8,128)}, f32[10,16,2,512]{3,1,2,0:T(8,128)}, u32[]{:S(2)}, u32[]{:S(2)}) collective-permute-start(f32[10,16,2,512]{3,1,2,0:T(8,128)} %get-tuple-element.32), channel_id=1, source_target_pairs={{1,0},{2,1},{3,2},{4,3},{5,4},{6,5},{7,6},{8,7},{9,8},{10,9},{11,1... | collective-permute-start | bytes 1966088 | tf_op jit(solution)/shard_map/ppermute | solution.py:42
  (11 other events, 434.6 us)
